TPU v7x, 256 devices: a whole 4x4x8 slice. The times are simulated.
256 devices in a mesh: wave: 64 (over z, x, core), lev: 4 (over y).
Axes of the slice: x: 4, y: 4, z: 8, core: 2. Of those that a mesh axis runs over, the one named last changes fastest.
Arguments:
- coeffs: bfloat16 [1280, 192, 1280], P('wave', 'lev'), may hold values from -0.3125 to 0.3125
- legendre: bfloat16 [1280, 64, 1280], P('wave'), may hold values from -0.15625 to 0.15625
- wave_of_slot: int32 [1280], replicated, may hold values from 0 to 1279, each once
- lon_count: int32 [64], P('wave'), may hold values from 1280 to 5120, as said below
Outputs:
- grid_field: bfloat16 [96, 64, 5120], P(None, 'wave', 'lev')
Inputs may be any that keep to these rules, and one draw needn't show every extreme that they name: `lon_count`: each count is a multiple of 4; some latitude has exactly 5120.
All inputs are finite; a program needn't handle non-finite values.
Results may differ from a plain program's by a relative error of at most 0.0055.
Values may be sent and summed in bfloat16 or wider, within the bound.
A program may use at most 192 MiB of HBM per device.

v0:
```python
import math

import jax
import jax.numpy as jnp
from jax import lax
from jax.sharding import PartitionSpec as P

NLONMAX = 5120


TWO_PI = 2.0 * math.pi
FINE_SPAN = 64


def fourier_table(wavenum, lon_total, lon_start, tile_width):
    column = wavenum[:, None]
    coarse_count = tile_width // FINE_SPAN
    coarse_index = lon_start + FINE_SPAN * lax.iota(jnp.int32, coarse_count)[None, :]
    fine_index = lax.iota(jnp.int32, FINE_SPAN)[None, :]
    step_angle = TWO_PI / lon_total.astype(jnp.float32)
    coarse_angle = (column * coarse_index % lon_total).astype(jnp.float32) * step_angle
    fine_angle = (column * fine_index % lon_total).astype(jnp.float32) * step_angle
    cos_coarse = jnp.cos(coarse_angle)[:, :, None]
    sin_coarse = jnp.sin(coarse_angle)[:, :, None]
    cos_fine = jnp.cos(fine_angle)[:, None, :]
    sin_fine = jnp.sin(fine_angle)[:, None, :]
    cos_sum = (cos_coarse * cos_fine - sin_coarse * sin_fine).reshape(column.shape[0], tile_width)
    sin_sum = (sin_coarse * cos_fine + cos_coarse * sin_fine).reshape(column.shape[0], tile_width)
    lon_index = lon_start + lax.iota(jnp.int32, tile_width)[None, :]
    kept_mask = (2 * column <= lon_total - 1) & (lon_index < lon_total)
    weight = jnp.where(column == 0, jnp.float32(1.0), jnp.float32(2.0))
    factor = jnp.where(kept_mask, weight, jnp.float32(0.0))
    cos_part = (factor * cos_sum).astype(jnp.bfloat16)
    sin_part = (-factor * sin_sum).astype(jnp.bfloat16)
    return jnp.stack([cos_part, sin_part])


def synthesis(lat_row, lon_total, wave_of_slot, lon_start, tile_width):
    twiddle = fourier_table(wave_of_slot, lon_total, lon_start, tile_width)
    paired = lat_row.reshape(lat_row.shape[0], -1, 2)
    result = jnp.einsum("sfc,csi->fi", paired, twiddle, preferred_element_type=jnp.float32)
    return result.astype(jnp.bfloat16)


def per_device(coeffs, legendre, wave_of_slot, lon_count):
    slot_count = coeffs.shape[0]
    total_waves = wave_of_slot.shape[0]
    first_slot = lax.axis_index("wave") * slot_count
    my_waves = lax.dynamic_slice_in_dim(wave_of_slot, first_slot, slot_count)
    degree_off = lax.iota(jnp.int32, total_waves)
    valid_mask = degree_off[None, :] < (total_waves - my_waves)[:, None]
    masked = coeffs * valid_mask[:, None, :].astype(coeffs.dtype)
    band_rows = jnp.einsum(
        "slk,sck->slc", legendre, masked, preferred_element_type=jnp.float32
    ).astype(jnp.bfloat16)
    spread = lax.all_to_all(band_rows, "wave", split_axis=1, concat_axis=0, tiled=True)
    lat_rows = spread.shape[1]
    tile_count = lax.axis_size("lev")
    tile_width = NLONMAX // tile_count
    gathered = lax.all_gather(spread, "lev", axis=2, tiled=True)
    tile_start = lax.axis_index("lev") * tile_width
    lat_parts = [synthesis(gathered[:, 0, :], lon_count[0], wave_of_slot, tile_start, tile_width)]
    return jnp.stack(lat_parts, axis=1)


def solution(mesh):
    return jax.shard_map(
        per_device,
        mesh=mesh,
        in_specs=(P("wave", "lev", None), P("wave", None, None), P(), P("wave")),
        out_specs=P(None, "wave", "lev"),
        check_vma=False,
    )
```

profile of v0, /device:TPU:8, one launch (start us, length us, event | category | flops | bytes accessed | tf_op | source)
XLA Modules:
  0.0 84.1 jit_solution(18424103234233433063)
XLA Ops:
  0.0 0.0 copy-start
  0.0 0.0 copy-start.1
  0.0 0.9 %dynamic-slice_subtract_fusion = s32[20]{0:T(128)S(1)} fusion(s32[1280]{0:T(1024)} %param.6, s32[]{:T(128)S(6)} %select_n.52), kind=kLoop, calls=%fused_computation.46 | loop fusion | flops 20 | bytes 164 | tf_op jit(solution)/shard_map/sub | solution.py:51
  0.9 0.1 fusion.42
  1.0 0.9 %copy-done = bf16[20,64,1280]{2,1,0:T(8,128)(2,1)S(1)} copy-done((bf16[20,64,1280]{2,1,0:T(8,128)(2,1)S(1)}, bf16[20,64,1280]{2,1,0:T(8,128)(2,1)}, u32[]{:S(2)}) %copy-start) | copy-done | bytes 3276824
  1.9 2.7 %fusion.22 = bf16[20,64,48]{1,2,0:T(8,128)(2,1)S(1)} fusion(bf16[20,64,1280]{2,1,0:T(8,128)(2,1)S(1)} %copy-done, bf16[20,48,1280]{2,1,0:T(8,128)(2,1)} %param.4, bf16[20,1280]{1,0:T(8,128)(2,1)S(1)} %fusion.42), kind=kOutput, calls=%fused_computation.18 | convolution fusion | flops 158576640 | bytes 5908480 | tf_op jit(solution)/shard_map/slk,sck->slc/dot_general | solution.py:53
  4.6 1.0 %copy.10 = bf16[20,64,48]{2,0,1:T(8,128)(2,1)} copy(bf16[20,64,48]{1,2,0:T(8,128)(2,1)S(1)} %fusion.22) | data formatting | bytes 245760 | tf_op jit(solution)/shard_map/convert_element_type | solution.py:55
  5.6 2.0 %reshape.362 = bf16[64,2,480]{2,1,0:T(2,128)(2,1)} reshape(bf16[64,20,48]{2,1,0:T(8,128)(2,1)} %bitcast.32) | data formatting | bytes 245760
  7.7 12.1 %all-to-all-start = ((bf16[64,2,480]{2,1,0:T(2,128)(2,1)}), bf16[64,2,480]{2,1,0:T(2,128)(2,1)S(1)}, u32[]{:S(2)}, u32[]{:S(2)}) async-start(bf16[64,2,480]{2,1,0:T(2,128)(2,1)} %reshape.362), calls=%async_computation | async-start | bytes 262144 | tf_op jit(solution)/shard_map/all_to_all | solution.py:56
  19.8 0.0 copy-done.1
  20.5 4.3 %fusion.31 = (f32[1280,64]{0,1:T(8,128)S(1)}, f32[1280,64]{0,1:T(8,128)S(1)}) fusion(f32[]{:T(128)S(6)} %div.3, s32[]{:T(128)S(6)} %select_n.55, s32[1280]{0:T(1024)S(1)} %copy-done.1, pred[]{:T(512)S(6)} %lt.66), kind=kLoop, calls=%fused_computation.27 | loop fusion | flops 819200 | bytes 660489 | tf_op jit(solution)/shard_map/cos | solution.py:25
  24.8 1.7 %fusion.39 = (f32[1280,20]{0,1:T(8,128)S(1)}, f32[1280,20]{0,1:T(8,128)S(1)}) fusion(f32[]{:T(128)S(6)} %div.3, s32[]{:T(128)S(6)} %select_n.55, s32[20]{0:T(128)S(1)} %multiply_add_fusion.1, s32[1280]{0:T(1024)S(1)} %copy-done.1, pred[]{:T(512)S(6)} %lt.66), kind=kLoop, calls=%fused_computation.37 | loop fusion | flops 256000 | bytes 210009 | tf_op jit(solution)/shard_map/cos | solution.py:23
  26.6 6.6 %multiply_subtract_fusion = (f32[1280,20,64]{0,2,1:T(8,128)}, f32[1280,20,64]{0,2,1:T(8,128)}) fusion(f32[1280,64]{0,1:T(8,128)S(1)} %get-tuple-element.12, f32[1280,20]{0,1:T(8,128)S(1)} %get-tuple-element.10, f32[1280,64]{0,1:T(8,128)S(1)} %get-tuple-element.11, f32[1280,20]{0,1:T(8,128)S(1)} %get-tuple-element.9), kind=kLoop, calls=%fused_computation.10 | loop fusion | flops 9830400 | bytes 13967360 | tf_op jit(solution)/shard_map/sub | solution.py:27
  33.2 8.2 %copy.12 = f32[1,1280,1280]{2,1,0:T(8,128)} copy(f32[1,1280,1280]{1,2,0:T(8,128)} %bitcast.31) | data formatting | bytes 13107200 | tf_op jit(solution)/shard_map/sub | solution.py:27
  41.3 8.2 %copy.13 = f32[1,1280,1280]{2,1,0:T(8,128)} copy(f32[1,1280,1280]{1,2,0:T(8,128)} %bitcast.30) | data formatting | bytes 13107200 | tf_op jit(solution)/shard_map/add | solution.py:28
  49.5 7.4 %fusion = (bf16[1,1280,1280]{2,1,0:T(8,128)(2,1)}, bf16[1,1280,1280]{2,1,0:T(8,128)(2,1)}) fusion(f32[1,1280,1280]{2,1,0:T(8,128)} %copy.12, f32[1280]{0:T(1024)S(1)} %compare_select_fusion, pred[1280]{0:T(1024)(128)(4,1)S(1)} %get-tuple-element.13, pred[1280]{0:T(1024)(128)(4,1)S(1)} %get-tuple-element.14, f32[1,1280,1280]{2,1,0:T(8,128)} %copy.13), kind=kLoop, calls=%fused_computation.2 | loop fusion | flops 11468800 | bytes 19668480 | tf_op jit(solution)/shard_map/convert_element_type | solution.py:33
  56.9 0.0 all-to-all-done
  56.9 1.2 %reshape.363 = bf16[64,20,48]{2,1,0:T(8,128)(2,1)} reshape(bf16[64,2,480]{2,1,0:T(2,128)(2,1)S(1)} %all-to-all-done) | data formatting | bytes 245760
  58.1 1.8 %bitcast_bitcast_fusion = bf16[64,20,1,48]{3,1,0,2:T(8,128)(2,1)} fusion(bf16[64,20,48]{2,1,0:T(8,128)(2,1)} %reshape.363), kind=kLoop, calls=%fused_computation.48 | loop fusion | bytes 245760 | tf_op jit(solution)/shard_map/all_to_all | solution.py:56
  59.9 1.8 %all_to_all.16 = bf16[1280,1,48]{2,0,1:T(8,128)(2,1)} reshape(bf16[64,20,1,48]{3,1,0,2:T(8,128)(2,1)} %bitcast_bitcast_fusion) | data formatting | bytes 245760 | tf_op jit(solution)/shard_map/all_to_all | solution.py:56
  61.7 1.1 %copy.11 = bf16[1280,1,48]{0,2,1:T(8,128)(2,1)S(1)} copy(bf16[1280,1,48]{2,0,1:T(8,128)(2,1)} %all_to_all.16) | data formatting | bytes 245760 | tf_op jit(solution)/shard_map/all_to_all | solution.py:56
  62.8 14.3 %all_gather.3 = bf16[1280,1,192]{0,2,1:T(8,128)(2,1)} all-gather(bf16[1280,1,48]{0,2,1:T(8,128)(2,1)S(1)} %copy.11), channel_id=1, replica_groups=mesh['wave'=64,'lev'=4] {'lev'}, dimensions={2}, use_global_device_ids=true | all-gather | bytes 614400 | tf_op jit(solution)/shard_map/all_gather | solution.py:60
  77.1 2.0 %reshape_squeeze.3 = bf16[1280,96,2]{0,2,1:T(2,128)(2,1)} reshape(bf16[1280,1,192]{0,2,1:T(8,128)(2,1)} %all_gather.3) | data formatting | bytes 983040 | tf_op jit(solution)/shard_map/reshape;squeeze | solution.py:40
  79.1 5.0 %fusion.15 = bf16[96,1,1280]{2,0,1:T(8,128)(2,1)} fusion(bf16[1,1280,1280]{2,1,0:T(8,128)(2,1)} %get-tuple-element.8, bf16[1,1280,1280]{2,1,0:T(8,128)(2,1)} %get-tuple-element.7, bf16[1280,96,2]{0,2,1:T(2,128)(2,1)} %reshape_squeeze.3), kind=kOutput, calls=%fused_computation.15 | convolution fusion | flops 632545280 | bytes 7290880 | tf_op jit(solution)/shard_map/sfc,csi->fi/dot_general | solution.py:41
  (3 shorter events, 0.0 us)
Async XLA Ops:
  0.0 1.9 %copy-start = (bf16[20,64,1280]{2,1,0:T(8,128)(2,1)S(1)}, bf16[20,64,1280]{2,1,0:T(8,128)(2,1)}, u32[]{:S(2)}) copy-start(bf16[20,64,1280]{2,1,0:T(8,128)(2,1)} %param.5) | copy-start | bytes 9830404
  0.0 19.8 %copy-start.1 = (s32[1280]{0:T(1024)S(1)}, s32[1280]{0:T(1024)}, u32[]{:S(2)}) copy-start(s32[1280]{0:T(1024)} %param.6) | copy-start | bytes 15364
  7.7 49.3 %all-to-all-start = ((bf16[64,2,480]{2,1,0:T(2,128)(2,1)}), bf16[64,2,480]{2,1,0:T(2,128)(2,1)S(1)}, u32[]{:S(2)}, u32[]{:S(2)}) async-start(bf16[64,2,480]{2,1,0:T(2,128)(2,1)} %reshape.362), calls=%async_computation | async-start | bytes 262144 | tf_op jit(solution)/shard_map/all_to_all | solution.py:56
where the time goes:
time: 84.8 us; the launch traced here: 84.1 us
  local copies, waits for them, and re-layouts  28.2 us (33%)
  other arithmetic  21.1 us (25%)
  blocking collectives  14.3 us (17%)
  starting transfers between devices  12.1 us (14%)
  matrix products  7.65 us (9%)
    all_gather x1, blocking collectives, per_device(): gathered = lax.all_gather(spread, 'lev', axis=2, tiled=True)  14.3 us
    all_to_all x1, starting transfers between devices, per_device(): lax.all_to_all(band_rows, 'wave', split_axis=1, concat_axis=0, tiled=True)  12.1 us
    add x1, local copies, waits for them, and re-layouts, fourier_table(): sin_coarse * cos_fine + cos_coarse * sin_fine  8.18 us
    sub x1, local copies, waits for them, and re-layouts, fourier_table(): cos_coarse * cos_fine - sin_coarse * sin_fine  8.17 us
    convert_element_type x1, other arithmetic, fourier_table(): cos_part = (factor * cos_sum).astype(jnp.bfloat16)  7.41 us
    sub x1, other arithmetic, fourier_table(): cos_coarse * cos_fine - sin_coarse * sin_fine  6.58 us
    dot_general x1, matrix products, synthesis(): jnp.einsum('sfc,csi->fi', paired, twiddle, preferred_element_type=jnp.flo...  4.97 us
    all_to_all x3, local copies, waits for them, and re-layouts, per_device(): lax.all_to_all(band_rows, 'wave', split_axis=1, concat_axis=0, tiled=True)  4.74 us
  transfers between devices with their start and end apart: 1, of which 0 were waited for; matrix products, arithmetic and copies ran while one was open for 43% of the time, Pallas kernels for 0%

commit v1 on v0

v1 whole, which is shorter than its diff:
```python
import functools

import jax
import jax.numpy as jnp
from jax import lax
from jax.experimental import pallas as pl
from jax.experimental.pallas import tpu as pltpu
from jax.sharding import PartitionSpec as P

MESH = pl.DeviceIdType.MESH
LANES = 128
ROWS = 8
HALF = 256
COS_POLY = (1.0, -4.934802055358887, 4.058712005615234, -1.335260272026062, 0.23532071709632874,
            -0.025785624980926514, 0.001904185046441853, -8.864672417985275e-05)
SIN_POLY = (3.1415927410125732, -5.167712688446045, 2.5501604080200195, -0.5992420315742493,
            0.08208133280277252, -0.00727477390319109, 0.0003950836544390768)


def horner(poly, square):
    total = jnp.full_like(square, poly[-1])
    for value in poly[-2::-1]:
        total = total * square + value
    return total


def cos_sin(product, total, inverse):
    turns = jnp.round(product * (0.5 * inverse))
    part = (product - turns * (2.0 * total)) * inverse
    square = part * part
    return horner(COS_POLY, square), part * horner(SIN_POLY, square)


def iota(shape, dim):
    return lax.broadcasted_iota(jnp.int32, shape, dim)


def kernel(waves, groups, slots, fields,
           coef_hbm, leg_hbm, wave_smem, count_smem, wave_row, out_ref,
           coef, leg, packed, send_buf, recv_buf, arrived, spectra, wave_of_lane,
           fine_cos, fine_sin, coarse_cos, coarse_sin, mid_cos, mid_sin,
           table_cos, table_sin, real_part, imag_part, tile_buf,
           coef_sem, leg_sem, wave_send, wave_recv, lev_send, lev_recv):
    me = lax.axis_index("wave")
    group = lax.axis_index("lev")
    parts = 2 * fields
    degrees = coef.shape[2]
    kblocks = slots // 2
    width = out_ref.shape[2]

    def fetch(s):
        return (pltpu.make_async_copy(coef_hbm.at[s], coef.at[s], coef_sem.at[s]),
                pltpu.make_async_copy(leg_hbm.at[s], leg.at[s], leg_sem.at[s]))

    order = []
    for r in range(ROWS):
        order += [r, ROWS + r] + ([2 * ROWS + r] if r < slots - 2 * ROWS else [])
    for s in order:
        for copy in fetch(s):
            copy.start()

    barrier = pltpu.get_barrier_semaphore()

    @pl.loop(1, waves)
    def _(j):
        pl.semaphore_signal(barrier, inc=1, device_id=(lax.rem(me + j, waves), group), device_id_type=MESH)

    for j in range(1, groups):
        pl.semaphore_signal(barrier, inc=1, device_id=(me, lax.rem(group + j, groups)), device_id_type=MESH)

    degree = iota((1, degrees), 1)
    rest = slots - 2 * ROWS

    def legendre(s):
        for copy in fetch(s):
            copy.wait()
        limit = waves * slots - wave_smem[me * slots + s]
        mask = jnp.where(degree < limit, 1.0, 0.0).astype(jnp.bfloat16)
        return lax.dot_general(leg[s], coef[s] * mask, (((1,), (1,)), ((), ())),
                               preferred_element_type=jnp.float32)

    third = {}
    for r in range(ROWS):
        first = legendre(r)
        second = legendre(ROWS + r)
        if r < rest:
            third[r] = legendre(2 * ROWS + r)
            tail = third[r][:, :32]
        else:
            tail = jnp.concatenate([third[r - rest][:, 32:], jnp.zeros((waves, 16), jnp.float32)], axis=1)
        packed[pl.ds(r, waves, stride=ROWS), :] = jnp.concatenate([first, second, tail], axis=1)
    send_buf[...] = packed[...].reshape(waves, ROWS, LANES).astype(jnp.bfloat16)
    recv_buf[me] = send_buf[me]

    pl.semaphore_wait(barrier, waves + groups - 2)

    @pl.loop(1, waves)
    def _(j):
        target = lax.rem(me + j, waves)
        pltpu.make_async_remote_copy(
            src_ref=send_buf.at[target], dst_ref=recv_buf.at[me], send_sem=wave_send, recv_sem=wave_recv,
            device_id=(target, group), device_id_type=MESH).start()

    numbers = wave_row[...].astype(jnp.float32)
    high = jnp.floor(numbers * 0.125)
    low = numbers - 8.0 * high
    total_slots = waves * slots
    slot_row = iota((16, total_slots), 1)
    slot_in = lax.rem(slot_row, slots)
    block_of = iota((16, total_slots), 0)
    picked = []
    for value in (high, low):
        for parity in (0, 1):
            picked.append(jnp.where(slot_in == 2 * block_of + parity, value, 0.0))
    source = iota((2 * waves, total_slots), 1) // slots
    spread = jnp.where(source == lax.rem(iota((2 * waves, total_slots), 0), waves), 1.0, 0.0)
    gathered = lax.dot_general(jnp.concatenate(picked, axis=0).astype(jnp.bfloat16), spread.astype(jnp.bfloat16),
                               (((1,), (1,)), ((), ())), preferred_element_type=jnp.float32)
    even = 8.0 * gathered[0:16] + gathered[32:48]
    odd = 8.0 * gathered[16:32] + gathered[48:64]
    wave_of_lane[...] = jnp.where(iota((16, LANES), 1) < waves, even, odd)

    count = count_smem[0].astype(jnp.float32)
    total = jnp.full((1, LANES), count, jnp.float32)
    inverse = 1.0 / total
    row16 = iota((16, LANES), 0)
    fine_step = (2 * row16 + 1).astype(jnp.float32)
    coarse_step = (32 * row16).astype(jnp.float32)
    tile_at = (row16 >= 3).astype(jnp.int32) + (row16 >= 6).astype(jnp.int32) + (row16 >= 9).astype(jnp.int32)
    centre = row16 - 3 * tile_at
    tile_of = lax.rem(group + 1 + tile_at, groups)
    mid_step = (2 * width * tile_of + jnp.where(centre == 0, HALF * 2 - 1, jnp.where(centre == 1, HALF * 6 - 1, HALF * 8 - 1)))
    mid_step = mid_step.astype(jnp.float32)

    def tables(kb):
        lanes = pl.ds(kb * LANES, LANES)
        m = jnp.broadcast_to(wave_of_lane[pl.ds(kb, 1), :], (16, LANES))
        fc, fs = cos_sin(m * fine_step, total, inverse)
        fine_cos[:, lanes] = fc
        fine_sin[:, lanes] = fs
        cc, cs = cos_sin(m * coarse_step, total, inverse)
        coarse_cos[:, lanes] = cc
        coarse_sin[:, lanes] = cs
        mc, ms = cos_sin(m * mid_step, total, inverse)
        factor = jnp.where(2.0 * m <= total - 1.0, jnp.where(m == 0.0, 1.0, 2.0), 0.0)
        mid_cos[:, lanes] = factor * mc
        mid_sin[:, lanes] = factor * ms
        for a in range(HALF // 16):
            ca = coarse_cos[pl.ds(a, 1), lanes]
            sa = coarse_sin[pl.ds(a, 1), lanes]
            table_cos[pl.ds(16 * a, 16), lanes] = (ca * fc - sa * fs).astype(jnp.bfloat16)
            table_sin[pl.ds(16 * a, 16), lanes] = (sa * fc + ca * fs).astype(jnp.bfloat16)

    for kb in range(kblocks):
        tables(kb)
    flip = jnp.where(iota((HALF, HALF), 0) + iota((HALF, HALF), 1) == HALF - 1, 1.0, 0.0).astype(jnp.bfloat16)

    bulk = pltpu.make_async_remote_copy(
        src_ref=send_buf.at[pl.ds(0, waves - 1)], dst_ref=recv_buf.at[pl.ds(0, waves - 1)],
        send_sem=wave_send, recv_sem=wave_recv, device_id=(me, group), device_id_type=MESH)
    bulk.wait_recv()

    arrived[...] = recv_buf[...].astype(jnp.float32).reshape(waves * ROWS, LANES)
    for j in range(ROWS // 2):
        rows = jnp.concatenate([arrived[pl.ds(2 * j, waves, stride=ROWS), :],
                                arrived[pl.ds(2 * j + 1, waves, stride=ROWS), :]], axis=0)
        turned = rows.T
        spectra[pl.ds(j * parts, parts), :] = turned[0:parts]
        spectra[pl.ds((ROWS // 2 + j) * parts, parts), :] = turned[parts:2 * parts]
        if j < rest // 2:
            spectra[pl.ds((ROWS + j) * parts, 32), :] = turned[96:128]
        else:
            spectra[pl.ds((ROWS + j - rest // 2) * parts + 32, 16), :] = turned[96:112]

    for kb in range(kblocks):
        lanes = pl.ds(kb * LANES, LANES)
        re = spectra[pl.ds(kb * parts, fields, stride=2), :]
        im = spectra[pl.ds(kb * parts + 1, fields, stride=2), :]
        for pair in range(3 * groups // 2):
            real, imag = [], []
            for at in (2 * pair, 2 * pair + 1):
                c = mid_cos[pl.ds(at, 1), lanes]
                s = mid_sin[pl.ds(at, 1), lanes]
                real.append(re * c - im * s)
                imag.append(re * s + im * c)
            rows = pl.ds(pair * parts, parts)
            real_part[rows, lanes] = jnp.concatenate(real, axis=0).astype(jnp.bfloat16)
            imag_part[rows, lanes] = jnp.concatenate(imag, axis=0).astype(jnp.bfloat16)

    dims = (((1,), (1,)), ((), ()))
    even_sum = lax.dot_general(real_part[...], table_cos[...], dims, preferred_element_type=jnp.float32)
    odd_sum = lax.dot_general(imag_part[...], table_sin[...], dims, preferred_element_type=jnp.float32)
    ahead = even_sum - odd_sum
    behind = jnp.dot((even_sum + odd_sum).astype(jnp.bfloat16), flip, preferred_element_type=jnp.float32)
    lane = iota((1, HALF), 1)
    limit = count_smem[0]

    def piece(tile, base, at, values):
        values = values[fields * (3 * tile + at):fields * (3 * tile + at + 1)]
        start = width * lax.rem(group + 1 + tile, groups) + base
        return jnp.where(lane + start < limit, values, 0.0).astype(jnp.bfloat16)

    sends = []
    for tile in range(groups):
        pieces = [piece(tile, 0, 0, behind), piece(tile, HALF, 0, ahead), piece(tile, 2 * HALF, 1, behind),
                  piece(tile, 3 * HALF, 1, ahead), piece(tile, 4 * HALF, 2, ahead)]
        result = jnp.concatenate(pieces, axis=1)
        if tile < groups - 1:
            tile_buf[tile] = result
            copy = pltpu.make_async_remote_copy(
                src_ref=tile_buf.at[tile], dst_ref=out_ref.at[group], send_sem=lev_send.at[tile],
                recv_sem=lev_recv.at[tile], device_id=(me, lax.rem(group + 1 + tile, groups)), device_id_type=MESH)
            copy.start()
            sends.append(copy)
        else:
            out_ref[group] = result
    bulk.wait_send()
    for tile, copy in enumerate(sends):
        copy.wait_send()
        sender = lax.rem(group + groups - 1 - tile, groups)
        pltpu.make_async_remote_copy(
            src_ref=tile_buf.at[tile], dst_ref=out_ref.at[sender], send_sem=lev_send.at[tile],
            recv_sem=lev_recv.at[tile], device_id=(me, sender), device_id_type=MESH).wait_recv()


def solution(mesh):
    waves, groups = mesh.shape["wave"], mesh.shape["lev"]

    def per_device(coeffs, legendre, wave_of_slot, lon_count):
        slots, parts, degrees = coeffs.shape
        lats = legendre.shape[1]
        fields = parts // 2
        width = 5120 // groups
        total = waves * slots
        centres = 3 * groups
        f32, bf16 = jnp.float32, jnp.bfloat16
        vmem = pl.BlockSpec(memory_space=pltpu.VMEM)
        smem = pl.BlockSpec(memory_space=pltpu.SMEM)
        hbm = pl.BlockSpec(memory_space=pl.ANY)
        dma = pltpu.SemaphoreType.DMA
        out = pl.pallas_call(
            functools.partial(kernel, waves, groups, slots, fields),
            out_shape=jax.ShapeDtypeStruct((groups, fields, width), bf16),
            in_specs=[hbm, hbm, smem, smem, vmem],
            out_specs=vmem,
            scratch_shapes=[
                pltpu.VMEM((slots, parts, degrees), bf16),
                pltpu.VMEM((slots, lats, degrees), bf16),
                pltpu.VMEM((waves * ROWS, LANES), f32),
                pltpu.VMEM((waves, ROWS, LANES), bf16),
                pltpu.VMEM((waves, ROWS, LANES), bf16),
                pltpu.VMEM((waves * ROWS, LANES), f32),
                pltpu.VMEM((slots // 2 * parts, LANES), f32),
                pltpu.VMEM((16, LANES), f32),
                pltpu.VMEM((16, total), f32), pltpu.VMEM((16, total), f32),
                pltpu.VMEM((16, total), f32), pltpu.VMEM((16, total), f32),
                pltpu.VMEM((16, total), f32), pltpu.VMEM((16, total), f32),
                pltpu.VMEM((HALF, total), bf16), pltpu.VMEM((HALF, total), bf16),
                pltpu.VMEM((centres * fields, total), bf16), pltpu.VMEM((centres * fields, total), bf16),
                pltpu.VMEM((groups - 1, fields, width), bf16),
                dma((slots,)), dma((slots,)), dma, dma, dma((groups - 1,)), dma((groups - 1,)),
            ],
            compiler_params=pltpu.CompilerParams(
                collective_id=0, has_side_effects=True, vmem_limit_bytes=40 * 2 ** 20),
        )(coeffs, legendre, wave_of_slot, lon_count, wave_of_slot.reshape(1, total))
        return out.reshape(groups * fields, 1, width)

    return jax.shard_map(
        per_device,
        mesh=mesh,
        in_specs=(P("wave", "lev", None), P("wave", None, None), P(), P("wave")),
        out_specs=P(None, "wave", "lev"),
        check_vma=False,
    )
```

time: 84.8 us -> 41.8 us (0.49)
  the two profiles are of different devices: /device:TPU:8 before, /device:TPU:1 now
where the time goes in v1:
time: 41.8 us; the launch traced here: 41.6 us
  Pallas kernels  35.2 us (84%)
  local copies, waits for them, and re-layouts  5.71 us (14%)
  between operations  0.66 us (2%)
    pallas_call x1, Pallas kernels, per_device(): pl.pallas_call(functools.partial(kernel, waves, groups, slots, fields), o...  35.2 us
    unnamed x7, local copies, waits for them, and re-layouts  5.01 us

profile of v1, /device:TPU:1, one launch (start us, length us, event | category | flops | bytes accessed | tf_op | source)
XLA Modules:
  0.0 41.6 jit_solution(12393799556378939144)
XLA Ops:
  0.7 0.7 %reshape.6.wave_row = s32[1,1280]{1,0:T(1,128)S(1)} reshape(s32[1280]{0:T(1024)} %wave_smem.1) | data formatting | bytes 10240 | tf_op jit(solution)/shard_map/reshape | solution.py:265
  1.4 0.0 copy-start
  1.4 1.9 %copy-done = bf16[20,64,1280]{2,1,0:T(8,128)(2,1)S(1)} copy-done((bf16[20,64,1280]{2,1,0:T(8,128)(2,1)S(1)}, bf16[20,64,1280]{2,1,0:T(8,128)(2,1)}, u32[]{:S(2)}) %copy-start) | copy-done | bytes 3276824
  3.3 0.0 copy-start.1
  3.3 1.7 %copy-done.1 = bf16[20,48,1280]{2,1,0:T(8,128)(2,1)S(1)} copy-done((bf16[20,48,1280]{2,1,0:T(8,128)(2,1)S(1)}, bf16[20,48,1280]{2,1,0:T(8,128)(2,1)}, u32[]{:S(2)}) %copy-start.1) | copy-done | bytes 2457624
  5.0 0.0 copy-start.2
  5.0 0.7 %copy-done.2 = s32[1280]{0:T(1024)S(1)} copy-done((s32[1280]{0:T(1024)S(1)}, s32[1280]{0:T(1024)}, u32[]{:S(2)}) %copy-start.2) | copy-done | bytes 5144
  5.7 35.2 %shard_map.46 = bf16[4,24,1280]{2,1,0:T(8,128)(2,1)S(1)} custom-call(bf16[20,48,1280]{2,1,0:T(8,128)(2,1)S(1)} %copy-done.1, bf16[20,64,1280]{2,1,0:T(8,128)(2,1)S(1)} %copy-done, s32[1280]{0:T(1024)S(1)} %copy-done.2, s32[1]{0:T(128)S(6)} %copy.6.count_smem, s32[1,1280]{1,0:T(1,128)S(1)} %reshape.6.wave_row), custom_call_target="tpu_custom_call" | custom-call | tf_op jit(solution)/shard_map/pallas_call | solution.py:241
  40.9 0.7 %copy.7 = bf16[96,1,1280]{2,0,1:T(8,128)(2,1)} copy(bf16[96,1,1280]{2,0,1:T(8,128)(2,1)S(1)} %bitcast.1) | data formatting | bytes 491520
Async XLA Ops:
  1.4 1.9 %copy-start = (bf16[20,64,1280]{2,1,0:T(8,128)(2,1)S(1)}, bf16[20,64,1280]{2,1,0:T(8,128)(2,1)}, u32[]{:S(2)}) copy-start(bf16[20,64,1280]{2,1,0:T(8,128)(2,1)} %leg_hbm.1) | copy-start | bytes 9830404
  3.3 1.7 %copy-start.1 = (bf16[20,48,1280]{2,1,0:T(8,128)(2,1)S(1)}, bf16[20,48,1280]{2,1,0:T(8,128)(2,1)}, u32[]{:S(2)}) copy-start(bf16[20,48,1280]{2,1,0:T(8,128)(2,1)} %coef_hbm.1) | copy-start | bytes 7372804
  5.0 0.7 %copy-start.2 = (s32[1280]{0:T(1024)S(1)}, s32[1280]{0:T(1024)}, u32[]{:S(2)}) copy-start(s32[1280]{0:T(1024)} %wave_smem.1) | copy-start | bytes 15364

commit v2 on v1

--- a/solution.py
+++ b/solution.py
@@ -11,10 +11,18 @@
 LANES = 128
 ROWS = 8
 HALF = 256
+GROUP = 2
 COS_POLY = (1.0, -4.934802055358887, 4.058712005615234, -1.335260272026062, 0.23532071709632874,
             -0.025785624980926514, 0.001904185046441853, -8.864672417985275e-05)
 SIN_POLY = (3.1415927410125732, -5.167712688446045, 2.5501604080200195, -0.5992420315742493,
             0.08208133280277252, -0.00727477390319109, 0.0003950836544390768)
+
+
+def peers(me):
+    steps = [(dz, dx, dc) for dz in range(8) for dx in range(4) for dc in range(2)][1:]
+    steps.sort(key=lambda d: -(2 * min(d[0], 8 - d[0]) + 2 * min(d[1], 4 - d[1]) + d[2]))
+    z, x, core = me // 8, lax.rem(me // 2, 4), lax.rem(me, 2)
+    return [8 * lax.rem(z + dz, 8) + 2 * lax.rem(x + dx, 4) + (1 - core if dc else core) for dz, dx, dc in steps]
 
 
 def horner(poly, square):
@@ -36,11 +44,11 @@
 
 
 def kernel(waves, groups, slots, fields,
-           coef_hbm, leg_hbm, wave_smem, count_smem, wave_row, out_ref,
-           coef, leg, packed, send_buf, recv_buf, arrived, spectra, wave_of_lane,
+           coef_hbm, leg_hbm, wave_hbm, count_smem, out_ref,
+           wave_smem, wave_rows, coef, leg, packed, send_buf, recv_buf, arrived, spectra, wave_of_lane,
            fine_cos, fine_sin, coarse_cos, coarse_sin, mid_cos, mid_sin,
            table_cos, table_sin, real_part, imag_part, tile_buf,
-           coef_sem, leg_sem, wave_send, wave_recv, lev_send, lev_recv):
+           wave_sem, coef_sem, leg_sem, wave_send, wave_recv, lev_send, lev_recv):
     me = lax.axis_index("wave")
     group = lax.axis_index("lev")
     parts = 2 * fields
@@ -48,39 +56,51 @@
     kblocks = slots // 2
     width = out_ref.shape[2]
 
-    def fetch(s):
-        return (pltpu.make_async_copy(coef_hbm.at[s], coef.at[s], coef_sem.at[s]),
-                pltpu.make_async_copy(leg_hbm.at[s], leg.at[s], leg_sem.at[s]))
-
-    order = []
-    for r in range(ROWS):
-        order += [r, ROWS + r] + ([2 * ROWS + r] if r < slots - 2 * ROWS else [])
-    for s in order:
-        for copy in fetch(s):
+    rest = slots - 2 * ROWS
+
+    def fetch(g):
+        starts = [2 * g, ROWS + 2 * g] + ([2 * ROWS + 2 * g] if 2 * g < rest else [])
+        for n, at in enumerate(starts):
+            two = pl.ds(at, 2)
+            yield pltpu.make_async_copy(coef_hbm.at[two], coef.at[two], coef_sem.at[g, n])
+            yield pltpu.make_async_copy(leg_hbm.at[two], leg.at[two], leg_sem.at[g, n])
+
+    to_smem = pltpu.make_async_copy(wave_hbm, wave_smem, wave_sem.at[0])
+    to_vmem = pltpu.make_async_copy(wave_hbm, wave_rows, wave_sem.at[1])
+    to_smem.start()
+    to_vmem.start()
+    for g in range(ROWS // 2):
+        for copy in fetch(g):
             copy.start()
 
     barrier = pltpu.get_barrier_semaphore()
 
-    @pl.loop(1, waves)
-    def _(j):
-        pl.semaphore_signal(barrier, inc=1, device_id=(lax.rem(me + j, waves), group), device_id_type=MESH)
+    for target in peers(me):
+        pl.semaphore_signal(barrier, inc=1, device_id=(target, group), device_id_type=MESH)
 
     for j in range(1, groups):
         pl.semaphore_signal(barrier, inc=1, device_id=(me, lax.rem(group + j, groups)), device_id_type=MESH)
 
+    to_smem.wait()
+    to_vmem.wait()
+
     degree = iota((1, degrees), 1)
-    rest = slots - 2 * ROWS
+    def number_of_slot(s):
+        place = me * slots + s
+        return wave_smem[place // LANES, lax.rem(place, LANES)]
 
     def legendre(s):
-        for copy in fetch(s):
-            copy.wait()
-        limit = waves * slots - wave_smem[me * slots + s]
+        limit = waves * slots - number_of_slot(s)
         mask = jnp.where(degree < limit, 1.0, 0.0).astype(jnp.bfloat16)
         return lax.dot_general(leg[s], coef[s] * mask, (((1,), (1,)), ((), ())),
                                preferred_element_type=jnp.float32)
 
     third = {}
     for r in range(ROWS):
+        if r % GROUP == 0:
+            for g in range(r // 2, (r + GROUP) // 2):
+                for copy in fetch(g):
+                    copy.wait()
         first = legendre(r)
         second = legendre(ROWS + r)
         if r < rest:
@@ -94,28 +114,27 @@
 
     pl.semaphore_wait(barrier, waves + groups - 2)
 
-    @pl.loop(1, waves)
-    def _(j):
-        target = lax.rem(me + j, waves)
+
+    for target in peers(me):
         pltpu.make_async_remote_copy(
             src_ref=send_buf.at[target], dst_ref=recv_buf.at[me], send_sem=wave_send, recv_sem=wave_recv,
             device_id=(target, group), device_id_type=MESH).start()
 
-    numbers = wave_row[...].astype(jnp.float32)
+    numbers = wave_rows[...].astype(jnp.float32)
     high = jnp.floor(numbers * 0.125)
     low = numbers - 8.0 * high
-    total_slots = waves * slots
-    slot_row = iota((16, total_slots), 1)
-    slot_in = lax.rem(slot_row, slots)
-    block_of = iota((16, total_slots), 0)
-    picked = []
-    for value in (high, low):
-        for parity in (0, 1):
-            picked.append(jnp.where(slot_in == 2 * block_of + parity, value, 0.0))
-    source = iota((2 * waves, total_slots), 1) // slots
-    spread = jnp.where(source == lax.rem(iota((2 * waves, total_slots), 0), waves), 1.0, 0.0)
-    gathered = lax.dot_general(jnp.concatenate(picked, axis=0).astype(jnp.bfloat16), spread.astype(jnp.bfloat16),
-                               (((1,), (1,)), ((), ())), preferred_element_type=jnp.float32)
+    block_of = iota((16, LANES), 0)
+    lane_of = iota((2 * waves, LANES), 0)
+    gathered = jnp.zeros((64, 2 * waves), jnp.float32)
+    for row in range(kblocks):
+        slot_of = iota((1, LANES), 1) + row * LANES
+        source = slot_of // slots
+        slot_in = slot_of - slots * source
+        picked = [jnp.where(slot_in == 2 * block_of + parity, value[row:row + 1], 0.0)
+                  for value in (high, low) for parity in (0, 1)]
+        spread = jnp.where((source == lane_of) | (source + waves == lane_of), 1.0, 0.0)
+        gathered += lax.dot_general(jnp.concatenate(picked, axis=0).astype(jnp.bfloat16), spread.astype(jnp.bfloat16),
+                                    (((1,), (1,)), ((), ())), preferred_element_type=jnp.float32)
     even = 8.0 * gathered[0:16] + gathered[32:48]
     odd = 8.0 * gathered[16:32] + gathered[48:64]
     wave_of_lane[...] = jnp.where(iota((16, LANES), 1) < waves, even, odd)
@@ -236,14 +255,16 @@
         f32, bf16 = jnp.float32, jnp.bfloat16
         vmem = pl.BlockSpec(memory_space=pltpu.VMEM)
         smem = pl.BlockSpec(memory_space=pltpu.SMEM)
-        hbm = pl.BlockSpec(memory_space=pl.ANY)
+        hbm = pl.BlockSpec(memory_space=pltpu.HBM)
         dma = pltpu.SemaphoreType.DMA
         out = pl.pallas_call(
             functools.partial(kernel, waves, groups, slots, fields),
             out_shape=jax.ShapeDtypeStruct((groups, fields, width), bf16),
-            in_specs=[hbm, hbm, smem, smem, vmem],
+            in_specs=[hbm, hbm, hbm, smem],
             out_specs=vmem,
             scratch_shapes=[
+                pltpu.SMEM((total // LANES, LANES), jnp.int32),
+                pltpu.VMEM((total // LANES, LANES), jnp.int32),
                 pltpu.VMEM((slots, parts, degrees), bf16),
                 pltpu.VMEM((slots, lats, degrees), bf16),
                 pltpu.VMEM((waves * ROWS, LANES), f32),
@@ -258,11 +279,12 @@
                 pltpu.VMEM((HALF, total), bf16), pltpu.VMEM((HALF, total), bf16),
                 pltpu.VMEM((centres * fields, total), bf16), pltpu.VMEM((centres * fields, total), bf16),
                 pltpu.VMEM((groups - 1, fields, width), bf16),
-                dma((slots,)), dma((slots,)), dma, dma, dma((groups - 1,)), dma((groups - 1,)),
+                dma((2,)), dma((ROWS // 2, 3)), dma((ROWS // 2, 3)), dma, dma, dma((groups - 1,)), dma((groups - 1,)),
             ],
             compiler_params=pltpu.CompilerParams(
-                collective_id=0, has_side_effects=True, vmem_limit_bytes=40 * 2 ** 20),
-        )(coeffs, legendre, wave_of_slot, lon_count, wave_of_slot.reshape(1, total))
+                collective_id=0, has_side_effects=True,
+ vmem_limit_bytes=53 * 2 ** 20),
+        )(coeffs, legendre, pltpu.with_memory_space_constraint(wave_of_slot.reshape(total // LANES, LANES), pltpu.HBM), lon_count)
         return out.reshape(groups * fields, 1, width)
 
     return jax.shard_map(

time: 41.8 us -> 25.3 us (0.61)
  Pallas kernels: 35.2 us -> 23.9 us
  local copies, waits for them, and re-layouts: 5.71 us -> 0.7 us
    pallas_call x1, Pallas kernels: 35.2 us -> 23.9 us  [per_device(): pl.pallas_call(functools.partial(kernel, waves, groups, slots, fields), o...]
    unnamed x7 -> x1, local copies, waits for them, and re-layouts: 5.01 us -> 0.7 us
    reshape x1 -> x0, local copies, waits for them, and re-layouts: 0.7 us -> none  [per_device(): wave_of_slot.reshape(1, total)]
where the time goes in v2:
time: 25.3 us; the launch traced here: 25.2 us
  Pallas kernels  23.9 us (94%)
  local copies, waits for them, and re-layouts  0.7 us (3%)
  between operations  0.66 us (3%)
    pallas_call x1, Pallas kernels, per_device(): pl.pallas_call(functools.partial(kernel, waves, groups, slots, fields), o...  23.9 us
    unnamed x1, local copies, waits for them, and re-layouts  0.7 us

profile of v2, /device:TPU:1, one launch (start us, length us, event | category | flops | bytes accessed | tf_op | source)
XLA Modules:
  0.0 25.2 jit_solution(16794540810086467154)
XLA Ops:
  0.7 23.9 %shard_map.46 = bf16[4,24,1280]{2,1,0:T(8,128)(2,1)S(1)} custom-call(bf16[20,48,1280]{2,1,0:T(8,128)(2,1)} %coef_hbm.1, bf16[20,64,1280]{2,1,0:T(8,128)(2,1)} %leg_hbm.1, s32[10,128]{1,0:T(8,128)} %bitcast.3, s32[1]{0:T(128)S(6)} %copy.6.count_smem), custom_call_target="tpu_custom_call" | custom-call | tf_op jit(solution)/shard_map/pallas_call | solution.py:260
  24.5 0.7 %copy.7 = bf16[96,1,1280]{2,0,1:T(8,128)(2,1)} copy(bf16[96,1,1280]{2,0,1:T(8,128)(2,1)S(1)} %bitcast.2) | data formatting | bytes 491520

commit v3 on v2

--- a/solution.py
+++ b/solution.py
@@ -18,11 +18,9 @@
             0.08208133280277252, -0.00727477390319109, 0.0003950836544390768)
 
 
-def peers(me):
-    steps = [(dz, dx, dc) for dz in range(8) for dx in range(4) for dc in range(2)][1:]
-    steps.sort(key=lambda d: -(2 * min(d[0], 8 - d[0]) + 2 * min(d[1], 4 - d[1]) + d[2]))
-    z, x, core = me // 8, lax.rem(me // 2, 4), lax.rem(me, 2)
-    return [8 * lax.rem(z + dz, 8) + 2 * lax.rem(x + dx, 4) + (1 - core if dc else core) for dz, dx, dc in steps]
+LATE_Z = (0, 2, 4, 7, 14, 14, 14, 14)
+LATE_X = (0, 3, 5, 3)
+WAVE_ORDER = sorted(range(64), key=lambda w: (LATE_Z[w // 8] + LATE_X[w // 2 % 4], -(w % 2), w))
 
 
 def horner(poly, square):
@@ -75,8 +73,10 @@
 
     barrier = pltpu.get_barrier_semaphore()
 
-    for target in peers(me):
-        pl.semaphore_signal(barrier, inc=1, device_id=(target, group), device_id_type=MESH)
+    for target in WAVE_ORDER:
+        @pl.when(me != target)
+        def _():
+            pl.semaphore_signal(barrier, inc=1, device_id=(target, group), device_id_type=MESH)
 
     for j in range(1, groups):
         pl.semaphore_signal(barrier, inc=1, device_id=(me, lax.rem(group + j, groups)), device_id_type=MESH)
@@ -115,10 +115,12 @@
     pl.semaphore_wait(barrier, waves + groups - 2)
 
 
-    for target in peers(me):
-        pltpu.make_async_remote_copy(
-            src_ref=send_buf.at[target], dst_ref=recv_buf.at[me], send_sem=wave_send, recv_sem=wave_recv,
-            device_id=(target, group), device_id_type=MESH).start()
+    for target in WAVE_ORDER:
+        @pl.when(me != target)
+        def _():
+            pltpu.make_async_remote_copy(
+                src_ref=send_buf.at[target], dst_ref=recv_buf.at[me], send_sem=wave_send, recv_sem=wave_recv,
+                device_id=(target, group), device_id_type=MESH).start()
 
     numbers = wave_rows[...].astype(jnp.float32)
     high = jnp.floor(numbers * 0.125)
@@ -152,7 +154,7 @@
     mid_step = mid_step.astype(jnp.float32)
 
     def tables(kb):
-        lanes = pl.ds(kb * LANES, LANES)
+        lanes = pl.ds(pl.multiple_of(kb * LANES, LANES), LANES)
         m = jnp.broadcast_to(wave_of_lane[pl.ds(kb, 1), :], (16, LANES))
         fc, fs = cos_sin(m * fine_step, total, inverse)
         fine_cos[:, lanes] = fc
@@ -170,8 +172,7 @@
             table_cos[pl.ds(16 * a, 16), lanes] = (ca * fc - sa * fs).astype(jnp.bfloat16)
             table_sin[pl.ds(16 * a, 16), lanes] = (sa * fc + ca * fs).astype(jnp.bfloat16)
 
-    for kb in range(kblocks):
-        tables(kb)
+    pl.loop(0, kblocks)(tables)
     flip = jnp.where(iota((HALF, HALF), 0) + iota((HALF, HALF), 1) == HALF - 1, 1.0, 0.0).astype(jnp.bfloat16)
 
     bulk = pltpu.make_async_remote_copy(

time: 25.3 us -> 24.4 us (0.964)
  Pallas kernels: 23.9 us -> 23 us
    pallas_call x1, Pallas kernels: 23.9 us -> 23 us  [per_device(): pl.pallas_call(functools.partial(kernel, waves, groups, slots, fields), o...]
where the time goes in v3:
time: 24.4 us; the launch traced here: 24.3 us
  Pallas kernels  23 us (94%)
  local copies, waits for them, and re-layouts  0.7 us (3%)
  between operations  0.66 us (3%)
    pallas_call x1, Pallas kernels, per_device(): pl.pallas_call(functools.partial(kernel, waves, groups, slots, fields), o...  23 us
    unnamed x1, local copies, waits for them, and re-layouts  0.7 us

profile of v3, /device:TPU:1, one launch (start us, length us, event | category | flops | bytes accessed | tf_op | source)
XLA Modules:
  0.0 24.3 jit_solution(440807597528132967)
XLA Ops:
  0.7 23.0 %shard_map.46 = bf16[4,24,1280]{2,1,0:T(8,128)(2,1)S(1)} custom-call(bf16[20,48,1280]{2,1,0:T(8,128)(2,1)} %coef_hbm.1, bf16[20,64,1280]{2,1,0:T(8,128)(2,1)} %leg_hbm.1, s32[10,128]{1,0:T(8,128)} %bitcast.3, s32[1]{0:T(128)S(6)} %copy.6.count_smem), custom_call_target="tpu_custom_call" | custom-call | tf_op jit(solution)/shard_map/pallas_call | solution.py:261
  23.7 0.7 %copy.7 = bf16[96,1,1280]{2,0,1:T(8,128)(2,1)} copy(bf16[96,1,1280]{2,0,1:T(8,128)(2,1)S(1)} %bitcast.2) | data formatting | bytes 491520

commit v4 on v3

--- a/solution.py
+++ b/solution.py
@@ -11,7 +11,7 @@
 LANES = 128
 ROWS = 8
 HALF = 256
-GROUP = 2
+STEPS = ((0, 4), (4, 4))
 COS_POLY = (1.0, -4.934802055358887, 4.058712005615234, -1.335260272026062, 0.23532071709632874,
             -0.025785624980926514, 0.001904185046441853, -8.864672417985275e-05)
 SIN_POLY = (3.1415927410125732, -5.167712688446045, 2.5501604080200195, -0.5992420315742493,
@@ -42,8 +42,8 @@
 
 
 def kernel(waves, groups, slots, fields,
-           coef_hbm, leg_hbm, wave_hbm, count_smem, out_ref,
-           wave_smem, wave_rows, coef, leg, packed, send_buf, recv_buf, arrived, spectra, wave_of_lane,
+           coef_hbm, leg_hbm, wave_hbm, count_hbm, out_ref,
+           count_smem, wave_smem, wave_rows, coef, leg, packed, send_buf, recv_buf, arrived, spectra, wave_of_lane,
            fine_cos, fine_sin, coarse_cos, coarse_sin, mid_cos, mid_sin,
            table_cos, table_sin, real_part, imag_part, tile_buf,
            wave_sem, coef_sem, leg_sem, wave_send, wave_recv, lev_send, lev_recv):
@@ -56,19 +56,22 @@
 
     rest = slots - 2 * ROWS
 
-    def fetch(g):
-        starts = [2 * g, ROWS + 2 * g] + ([2 * ROWS + 2 * g] if 2 * g < rest else [])
+    def fetch(step):
+        first, many = STEPS[step]
+        starts = [first, ROWS + first] + ([2 * ROWS + first] if first < rest else [])
         for n, at in enumerate(starts):
-            two = pl.ds(at, 2)
-            yield pltpu.make_async_copy(coef_hbm.at[two], coef.at[two], coef_sem.at[g, n])
-            yield pltpu.make_async_copy(leg_hbm.at[two], leg.at[two], leg_sem.at[g, n])
+            these = pl.ds(at, many)
+            yield pltpu.make_async_copy(coef_hbm.at[these], coef.at[these], coef_sem.at[step, n])
+            yield pltpu.make_async_copy(leg_hbm.at[these], leg.at[these], leg_sem.at[step, n])
 
     to_smem = pltpu.make_async_copy(wave_hbm, wave_smem, wave_sem.at[0])
     to_vmem = pltpu.make_async_copy(wave_hbm, wave_rows, wave_sem.at[1])
+    to_count = pltpu.make_async_copy(count_hbm, count_smem, wave_sem.at[2])
     to_smem.start()
     to_vmem.start()
-    for g in range(ROWS // 2):
-        for copy in fetch(g):
+    to_count.start()
+    for step in range(len(STEPS)):
+        for copy in fetch(step):
             copy.start()
 
     barrier = pltpu.get_barrier_semaphore()
@@ -83,6 +86,7 @@
 
     to_smem.wait()
     to_vmem.wait()
+    to_count.wait()
 
     degree = iota((1, degrees), 1)
     def number_of_slot(s):
@@ -97,9 +101,9 @@
 
     third = {}
     for r in range(ROWS):
-        if r % GROUP == 0:
-            for g in range(r // 2, (r + GROUP) // 2):
-                for copy in fetch(g):
+        for step, (start, _) in enumerate(STEPS):
+            if start == r:
+                for copy in fetch(step):
                     copy.wait()
         first = legendre(r)
         second = legendre(ROWS + r)
@@ -141,7 +145,7 @@
     odd = 8.0 * gathered[16:32] + gathered[48:64]
     wave_of_lane[...] = jnp.where(iota((16, LANES), 1) < waves, even, odd)
 
-    count = count_smem[0].astype(jnp.float32)
+    count = count_smem[0, 0].astype(jnp.float32)
     total = jnp.full((1, LANES), count, jnp.float32)
     inverse = 1.0 / total
     row16 = iota((16, LANES), 0)
@@ -213,7 +217,7 @@
     ahead = even_sum - odd_sum
     behind = jnp.dot((even_sum + odd_sum).astype(jnp.bfloat16), flip, preferred_element_type=jnp.float32)
     lane = iota((1, HALF), 1)
-    limit = count_smem[0]
+    limit = count_smem[0, 0]
 
     def piece(tile, base, at, values):
         values = values[fields * (3 * tile + at):fields * (3 * tile + at + 1)]
@@ -255,15 +259,15 @@
         centres = 3 * groups
         f32, bf16 = jnp.float32, jnp.bfloat16
         vmem = pl.BlockSpec(memory_space=pltpu.VMEM)
-        smem = pl.BlockSpec(memory_space=pltpu.SMEM)
         hbm = pl.BlockSpec(memory_space=pltpu.HBM)
         dma = pltpu.SemaphoreType.DMA
         out = pl.pallas_call(
             functools.partial(kernel, waves, groups, slots, fields),
             out_shape=jax.ShapeDtypeStruct((groups, fields, width), bf16),
-            in_specs=[hbm, hbm, hbm, smem],
+            in_specs=[hbm] * 4,
             out_specs=vmem,
             scratch_shapes=[
+                pltpu.SMEM((1, 1), jnp.int32),
                 pltpu.SMEM((total // LANES, LANES), jnp.int32),
                 pltpu.VMEM((total // LANES, LANES), jnp.int32),
                 pltpu.VMEM((slots, parts, degrees), bf16),
@@ -280,12 +284,13 @@
                 pltpu.VMEM((HALF, total), bf16), pltpu.VMEM((HALF, total), bf16),
                 pltpu.VMEM((centres * fields, total), bf16), pltpu.VMEM((centres * fields, total), bf16),
                 pltpu.VMEM((groups - 1, fields, width), bf16),
-                dma((2,)), dma((ROWS // 2, 3)), dma((ROWS // 2, 3)), dma, dma, dma((groups - 1,)), dma((groups - 1,)),
+                dma((3,)), dma((len(STEPS), 3)), dma((len(STEPS), 3)), dma, dma, dma((groups - 1,)), dma((groups - 1,)),
             ],
             compiler_params=pltpu.CompilerParams(
                 collective_id=0, has_side_effects=True,
  vmem_limit_bytes=53 * 2 ** 20),
-        )(coeffs, legendre, pltpu.with_memory_space_constraint(wave_of_slot.reshape(total // LANES, LANES), pltpu.HBM), lon_count)
+        )(coeffs, legendre, pltpu.with_memory_space_constraint(wave_of_slot.reshape(total // LANES, LANES), pltpu.HBM),
+          lon_count.reshape(1, 1))
         return out.reshape(groups * fields, 1, width)
 
     return jax.shard_map(

time: 24.4 us -> 23.9 us (0.980)
  Pallas kernels: 23 us -> 22.5 us
    pallas_call x1, Pallas kernels: 23 us -> 22.5 us  [per_device(): pl.pallas_call(functools.partial(kernel, waves, groups, slots, fields), o...]
where the time goes in v4:
time: 23.9 us
  Pallas kernels  22.5 us (94%)
  local copies, waits for them, and re-layouts  0.7 us (3%)
  between operations  0.66 us (3%)
    pallas_call x1, Pallas kernels, per_device(): pl.pallas_call(functools.partial(kernel, waves, groups, slots, fields), o...  22.5 us
    unnamed x1, local copies, waits for them, and re-layouts  0.7 us

profile of v4, /device:TPU:1, one launch (start us, length us, event | category | flops | bytes accessed | tf_op | source)
XLA Modules:
  0.0 23.9 jit_solution(439735694413558386)
XLA Ops:
  0.7 22.5 %shard_map.46 = bf16[4,24,1280]{2,1,0:T(8,128)(2,1)S(1)} custom-call(bf16[20,48,1280]{2,1,0:T(8,128)(2,1)} %coef_hbm.1, bf16[20,64,1280]{2,1,0:T(8,128)(2,1)} %leg_hbm.1, s32[10,128]{1,0:T(8,128)} %bitcast.5, s32[1,1]{1,0:T(1,128)} %bitcast.3.count_hbm), custom_call_target="tpu_custom_call" | custom-call | tf_op jit(solution)/shard_map/pallas_call | solution.py:264
  23.2 0.7 %copy.7 = bf16[96,1,1280]{2,0,1:T(8,128)(2,1)} copy(bf16[96,1,1280]{2,0,1:T(8,128)(2,1)S(1)} %bitcast.4) | data formatting | bytes 491520

commit v5 on v4

--- a/solution.py
+++ b/solution.py
@@ -18,9 +18,9 @@
             0.08208133280277252, -0.00727477390319109, 0.0003950836544390768)
 
 
-LATE_Z = (0, 2, 4, 7, 14, 14, 14, 14)
-LATE_X = (0, 3, 5, 3)
-WAVE_ORDER = sorted(range(64), key=lambda w: (LATE_Z[w // 8] + LATE_X[w // 2 % 4], -(w % 2), w))
+HOPS_Z = (0, 2, 4, 6, 8, 6, 4, 2)
+HOPS_X = (0, 2, 4, 2)
+WAVE_ORDER = sorted(range(64), key=lambda w: (HOPS_Z[w // 8] + HOPS_X[w // 2 % 4], -(w % 2), w))
 
 
 def horner(poly, square):
@@ -89,6 +89,7 @@
     to_count.wait()
 
     degree = iota((1, degrees), 1)
+
     def number_of_slot(s):
         place = me * slots + s
         return wave_smem[place // LANES, lax.rem(place, LANES)]
@@ -113,11 +114,10 @@
         else:
             tail = jnp.concatenate([third[r - rest][:, 32:], jnp.zeros((waves, 16), jnp.float32)], axis=1)
         packed[pl.ds(r, waves, stride=ROWS), :] = jnp.concatenate([first, second, tail], axis=1)
-    send_buf[...] = packed[...].reshape(waves, ROWS, LANES).astype(jnp.bfloat16)
+    send_buf[...] = packed[pl.ds(0, waves * ROWS), :].reshape(waves, ROWS, LANES).astype(jnp.bfloat16)
     recv_buf[me] = send_buf[me]
 
     pl.semaphore_wait(barrier, waves + groups - 2)
-
 
     for target in WAVE_ORDER:
         @pl.when(me != target)
@@ -184,7 +184,7 @@
         send_sem=wave_send, recv_sem=wave_recv, device_id=(me, group), device_id_type=MESH)
     bulk.wait_recv()
 
-    arrived[...] = recv_buf[...].astype(jnp.float32).reshape(waves * ROWS, LANES)
+    arrived[pl.ds(0, waves * ROWS), :] = recv_buf[...].astype(jnp.float32).reshape(waves * ROWS, LANES)
     for j in range(ROWS // 2):
         rows = jnp.concatenate([arrived[pl.ds(2 * j, waves, stride=ROWS), :],
                                 arrived[pl.ds(2 * j + 1, waves, stride=ROWS), :]], axis=0)
@@ -272,11 +272,11 @@
                 pltpu.VMEM((total // LANES, LANES), jnp.int32),
                 pltpu.VMEM((slots, parts, degrees), bf16),
                 pltpu.VMEM((slots, lats, degrees), bf16),
-                pltpu.VMEM((waves * ROWS, LANES), f32),
+                pltpu.VMEM((waves * ROWS + ROWS, LANES), f32),
                 pltpu.VMEM((waves, ROWS, LANES), bf16),
                 pltpu.VMEM((waves, ROWS, LANES), bf16),
-                pltpu.VMEM((waves * ROWS, LANES), f32),
-                pltpu.VMEM((slots // 2 * parts, LANES), f32),
+                pltpu.VMEM((waves * ROWS + ROWS, LANES), f32),
+                pltpu.VMEM((slots // 2 * parts + ROWS, LANES), f32),
                 pltpu.VMEM((16, LANES), f32),
                 pltpu.VMEM((16, total), f32), pltpu.VMEM((16, total), f32),
                 pltpu.VMEM((16, total), f32), pltpu.VMEM((16, total), f32),

time: 23.9 us -> 23.9 us (level)
  no operation moved by 1% of the time
where the time goes in v5:
time: 23.9 us; the launch traced here: 23.8 us
  Pallas kernels  22.5 us (94%)
  local copies, waits for them, and re-layouts  0.7 us (3%)
  between operations  0.66 us (3%)
    pallas_call x1, Pallas kernels, per_device(): pl.pallas_call(functools.partial(kernel, waves, groups, slots, fields), o...  22.5 us
    unnamed x1, local copies, waits for them, and re-layouts  0.7 us

profile of v5, /device:TPU:1, one launch (start us, length us, event | category | flops | bytes accessed | tf_op | source)
XLA Modules:
  0.0 23.8 jit_solution(2345767951973591722)
XLA Ops:
  0.7 22.5 %shard_map.46 = bf16[4,24,1280]{2,1,0:T(8,128)(2,1)S(1)} custom-call(bf16[20,48,1280]{2,1,0:T(8,128)(2,1)} %coef_hbm.1, bf16[20,64,1280]{2,1,0:T(8,128)(2,1)} %leg_hbm.1, s32[10,128]{1,0:T(8,128)} %bitcast.5, s32[1,1]{1,0:T(1,128)} %bitcast.3.count_hbm), custom_call_target="tpu_custom_call" | custom-call | tf_op jit(solution)/shard_map/pallas_call | solution.py:264
  23.1 0.7 %copy.7 = bf16[96,1,1280]{2,0,1:T(8,128)(2,1)} copy(bf16[96,1,1280]{2,0,1:T(8,128)(2,1)S(1)} %bitcast.4) | data formatting | bytes 491520
